TPU v7x, 1024 devices: a whole 8x8x8 slice. The times are simulated.
1024 devices in a mesh: rep: 16 (over x, core), fsdp: 64 (over z, y).
Axes of the slice: x: 8, y: 8, z: 8, core: 2. Of those that a mesh axis runs over, the one named last changes fastest.
Arguments:
- deltas: bfloat16 [16, 4096, 8192], P('rep', None, 'fsdp'), may hold values from -6 to 6
- sign_bits: int32 [16, 8192], replicated, may hold values from 0 to 1
- kept_tiles: int32 [16, 32], replicated, may hold values from 0 to 63, as said below
- kept_count: int32 [16], replicated, may hold values from 8 to 32, as said below
- params: float32 [4096, 8192], P(('fsdp', 'rep')), may hold values from -6 to 6
- momentum: float32 [4096, 8192], P(('fsdp', 'rep')), may hold values from -4 to 4
Outputs:
- new_params: float32 [4096, 8192], P(('fsdp', 'rep'))
- new_momentum: float32 [4096, 8192], P(('fsdp', 'rep'))
- working: bfloat16 [4096, 8192], P(None, 'fsdp')
Inputs may be any that keep to these rules, and one draw needn't show every extreme that they name: `kept_count`: how many tiles each replica keeps; some replica keeps exactly 32. `kept_tiles`: each row holds distinct tile numbers; the first kept_count[r] entries of row r name the tiles replica r keeps, the rest are unused.
All inputs are finite; a program needn't handle non-finite values.
Results may differ from a plain program's by a relative error of at most 0.0034.
Values may be sent and summed in bfloat16 or wider, within the bound.
A program may use at most 32 MiB of HBM per device.

v0:
```python
import math

import jax
import jax.numpy as jnp
from jax import lax
from jax.sharding import PartitionSpec as P

BLOCK = 1024
TILE = 128


def sylvester_signs(order):
    indices = jnp.arange(order, dtype=jnp.int32)
    intersection = indices[:, None] & indices[None, :]
    parity = jnp.zeros((order, order), jnp.int32)
    for bit_number in range(order.bit_length() - 1):
        parity = parity + (intersection >> bit_number & 1)
    return jnp.where(parity % 2 == 0, 1.0, -1.0).astype(jnp.float32)


def body(deltas, sign_bits, kept_tiles, kept_count, params, momentum):
    regrouped = lax.all_to_all(deltas, "fsdp", split_axis=1, concat_axis=2, tiled=True)
    row_block = regrouped[0]
    row_total = row_block.shape[0]
    width = row_block.shape[1]
    blocks = width // BLOCK
    tile_total = width // TILE
    owner_count = lax.axis_size("rep")
    my_replica = lax.axis_index("rep")
    rotation = (sylvester_signs(BLOCK) * (1.0 / math.sqrt(BLOCK))).astype(jnp.bfloat16)
    signs_all = (1 - 2 * sign_bits).astype(jnp.float32)
    slot_live = jnp.arange(kept_tiles.shape[1], dtype=jnp.int32)[None, :] < kept_count[:, None]
    placer = (
        kept_tiles[:, :, None] == jnp.arange(tile_total, dtype=jnp.int32)[None, None, :]
    ) & slot_live[:, :, None]
    factors = tile_total / kept_count.astype(jnp.float32)
    my_sign = lax.dynamic_index_in_dim(signs_all, my_replica, 0, keepdims=False)
    my_factor = lax.dynamic_index_in_dim(factors, my_replica, 0, keepdims=False)
    scaled_in = row_block * my_sign.astype(jnp.bfloat16)[None, :]
    rotated = jnp.einsum(
        "nbi,ij->nbj",
        scaled_in.reshape(row_total, blocks, BLOCK),
        rotation,
        preferred_element_type=jnp.float32,
    ).reshape(row_total, tile_total, TILE)
    my_placer = lax.dynamic_index_in_dim(placer, my_replica, 0, keepdims=False)
    mask_tiles = jnp.sum(my_placer.astype(jnp.float32), axis=0)
    weights = mask_tiles * my_factor
    kept = (rotated * weights[None, :, None]).astype(jnp.bfloat16).reshape(row_total, blocks, BLOCK)
    back = jnp.einsum("nbi,ij->nbj", kept, rotation, preferred_element_type=jnp.float32).reshape(
        row_total // owner_count * lax.axis_size("rep"), width
    )
    summed = lax.psum_scatter(back * my_sign[None, :], "rep", scatter_dimension=0, tiled=True)
    outer_grad = summed / owner_count
    new_momentum = 0.9 * momentum + outer_grad
    new_params = params - 0.7 * (outer_grad + 0.9 * new_momentum)
    working = new_params.astype(jnp.bfloat16)
    gathered = lax.all_gather(working, "rep", axis=0, tiled=True)
    full_rows = lax.all_to_all(gathered, "fsdp", split_axis=1, concat_axis=0, tiled=True)
    return (new_params, new_momentum, full_rows)


def solution(mesh):
    placed = (
        P("rep", None, "fsdp"),
        P(),
        P(),
        P(),
        P(("fsdp", "rep"), None),
        P(("fsdp", "rep"), None),
    )
    return jax.shard_map(
        body,
        mesh=mesh,
        in_specs=placed,
        out_specs=(P(("fsdp", "rep"), None), P(("fsdp", "rep"), None), P(None, "fsdp")),
        check_vma=False,
    )
```

profile of v0, /device:TPU:1, one launch (start us, length us, event | category | flops | bytes accessed | tf_op | source)
XLA Modules:
  0.0 322.9 jit_solution(16900749365077256360)
XLA Ops:
  7.2 3.2 copy.33
  10.4 0.5 broadcast.77
  10.9 22.4 %reduce.3 = bf16[4096,128]{1,0:T(8,128)(2,1)S(1)} reduce(bf16[4096,1,128]{2,1,0:T(2,128)(2,1)S(1)} %bitcast.31, bf16[]{:T(256)} %broadcast.77), dimensions={1}, to_apply=%bitcast.28.reduce_sub_computation | reduce | bytes 2097154
  33.3 1.1 reshape.62
  34.4 24.0 %all-to-all-start = ((bf16[64,2,4096]{2,1,0:T(2,128)(2,1)}), bf16[64,2,4096]{2,1,0:T(2,128)(2,1)S(1)}, u32[]{:S(2)}, u32[]{:S(2)}) async-start(bf16[64,2,4096]{2,1,0:T(2,128)(2,1)} %reshape.62), calls=%async_computation | async-start | bytes 2097152 | tf_op jit(solution)/shard_map/all_to_all | solution.py:22
  58.6 0.6 dynamic_slice.14
  59.4 0.6 broadcast_multiply_fusion.1
  60.2 1.1 convert_reduce_fusion
  61.4 24.4 %all-to-all-done = bf16[64,2,4096]{2,1,0:T(2,128)(2,1)S(1)} async-done(((bf16[64,2,4096]{2,1,0:T(2,128)(2,1)}), bf16[64,2,4096]{2,1,0:T(2,128)(2,1)S(1)}, u32[]{:S(2)}, u32[]{:S(2)}) %all-to-all-start) | async-done | bytes 1048608 | tf_op jit(solution)/shard_map/all_to_all | solution.py:22
  85.8 1.0 reshape.63
  87.0 0.7 copy.27
  87.7 0.5 squeeze.11
  88.2 8.2 %fusion.3 = f32[64,8,1024]{2,1,0:T(8,128)S(1)} fusion(f32[8,1024]{1,0:T(8,128)S(1)} %broadcast_bitcast_fusion, bf16[64,8,1024]{2,1,0:T(8,128)(2,1)S(1)} %squeeze.11, bf16[8,1024]{1,0:T(8,128)(2,1)S(1)} %mul.75), kind=kOutput, calls=%fused_computation.8 | convolution fusion | flops 2243428352 | bytes 3194880 | tf_op jit(solution)/shard_map/nbi,ij->nbj/dot_general | solution.py:50
  96.4 1.2 copy.31
  97.6 1.5 broadcast_multiply_fusion
  99.1 0.3 all-gather.3.cloned.1.call-start
  99.4 1.3 dynamic-slice
  101.3 120.8 %all-reduce.3.cloned.1.call-done = f32[64,8192]{1,0:T(8,128)} async-done(((f32[64,8192]{1,0:T(8,128)}), f32[64,8192]{1,0:T(8,128)}) %all-reduce.3.cloned.1.call-update) | async-done | bytes 2097168
  222.1 1.8 convert_bitcast_fusion
  223.9 46.7 %all-gather.3.cloned.1.call-done = bf16[16,4,8192]{2,1,0:T(4,128)(2,1)} async-done(((bf16[1,4,8192]{2,1,0:T(4,128)(2,1)}), bf16[16,4,8192]{2,1,0:T(4,128)(2,1)}) %all-gather.3.cloned.1.call-update) | async-done | bytes 1048592 | tf_op jit(solution)/shard_map/all_gather | solution.py:58
  270.6 2.1 all_to_all.28
  272.7 0.7 copy.29
  273.4 41.7 %all_to_all.34 = bf16[64,64,128]{2,0,1:T(8,128)(2,1)S(1)} all-to-all(bf16[64,64,128]{2,0,1:T(8,128)(2,1)S(1)} %copy.29), channel_id=1, replica_groups=mesh['rep'=16,'fsdp'=64] {'fsdp'}, dimensions={1} | all-to-all | bytes 2097152 | tf_op jit(solution)/shard_map/all_to_all | solution.py:59
  315.1 1.0 copy.36
  (21 shorter events, 0.8 us)
Async XLA Ops:
  7.2 52.1 %copy-start = (s32[16,32]{1,0:T(8,128)S(1)}, s32[16,32]{1,0:T(8,128)}, u32[]{:S(2)}) copy-start(s32[16,32]{1,0:T(8,128)} %param.8) | copy-start | bytes 6148
  33.3 25.3 %copy-start.3 = (s32[16]{0:T(128)S(1)}, s32[16]{0:T(128)}, u32[]{:S(2)}) copy-start(s32[16]{0:T(128)} %param.9) | copy-start | bytes 196
  34.4 51.4 %all-to-all-start = ((bf16[64,2,4096]{2,1,0:T(2,128)(2,1)}), bf16[64,2,4096]{2,1,0:T(2,128)(2,1)S(1)}, u32[]{:S(2)}, u32[]{:S(2)}) async-start(bf16[64,2,4096]{2,1,0:T(2,128)(2,1)} %reshape.62), calls=%async_computation | async-start | bytes 2097152 | tf_op jit(solution)/shard_map/all_to_all | solution.py:22
  58.4 163.7 %all-reduce.3.cloned.1.call-start = ((), (), s32[]{:S(2)}) async-start(), calls=%async_computation.3 | async-start | bytes 4194304
  99.1 123.0 %copy-start.1 = (f32[4,8192]{1,0:T(4,128)S(1)}, f32[4,8192]{1,0:T(4,128)}, u32[]{:S(2)}) copy-start(f32[4,8192]{1,0:T(4,128)} %param.10) | copy-start | bytes 393220
  99.1 123.0 %copy-start.2 = (f32[4,8192]{1,0:T(4,128)S(1)}, f32[4,8192]{1,0:T(4,128)}, u32[]{:S(2)}) copy-start(f32[4,8192]{1,0:T(4,128)} %param.11) | copy-start | bytes 393220
  99.1 171.5 %all-gather.3.cloned.1.call-start = ((), (), s32[]{:S(2)}) async-start(), calls=%async_computation.2 | async-start | bytes 1114112 | tf_op jit(solution)/shard_map/all_gather | solution.py:58
Sparse Core Ops, SparseCore 0:
  99.2 122.8 all-reduce.2
  225.3 45.1 all-gather.2
where the time goes:
time: 324 us; the launch traced here: 323 us
  waiting for transfers between devices  192 us (59%)
  blocking collectives  41.7 us (13%)
  other arithmetic  27.5 us (8%)
  starting transfers between devices  24.4 us (8%)
  between operations  14.8 us (5%)
  local copies, waits for them, and re-layouts  14.3 us (4%)
  matrix products  8.19 us (3%)
    unnamed x3, waiting for transfers between devices  121 us
    all_gather x1, waiting for transfers between devices, body(): gathered = lax.all_gather(working, 'rep', axis=0, tiled=True)  46.7 us
    all_to_all x1, blocking collectives, body(): lax.all_to_all(gathered, 'fsdp', split_axis=1, concat_axis=0, tiled=True)  41.7 us
    all_to_all x1, waiting for transfers between devices, body(): lax.all_to_all(deltas, 'fsdp', split_axis=1, concat_axis=2, tiled=True)  24.4 us
    unnamed x2, other arithmetic  24.2 us
    all_to_all x1, starting transfers between devices, body(): lax.all_to_all(deltas, 'fsdp', split_axis=1, concat_axis=2, tiled=True)  24 us
    unnamed x16, local copies, waits for them, and re-layouts  9.44 us
    dot_general x1, matrix products, body(): jnp.einsum('nbi,ij->nbj', kept, rotation, preferred_element_type=jnp.floa...  8.19 us
  transfers between devices with their start and end apart: 3, of which 3 were waited for; matrix products, arithmetic and copies ran while one was open for 1% of the time, Pallas kernels for 0%

commit v1 on v0

v1 whole, which is shorter than its diff:
```python
import jax
import jax.numpy as jnp
from jax import lax
from jax.experimental import pallas as pl
from jax.experimental.pallas import tpu as pltpu
from jax.sharding import PartitionSpec as P

MESH = pl.DeviceIdType.MESH
DMA = pltpu.SemaphoreType.DMA
CHUNKS = 4
NZ = 8 // CHUNKS
MOST = 32
F32 = jnp.float32
BF16 = jnp.bfloat16


def place():
    rep = lax.axis_index("rep")
    col = lax.axis_index("fsdp")
    return rep // 2, rep % 2, col % 8, col // 8


def at(x, c, y, z):
    return (2 * x + c, 8 * z + y)


def loop(low, high, body):
    def step(i, carry):
        body(i)
        return carry

    lax.fori_loop(low, high, step, jnp.int32(0))


def butterfly(v):
    for bit in (1, 2, 4):
        v = [v[i] + v[i | bit] if not i & bit else v[i ^ bit] - v[i] for i in range(8)]
    return v


def hadamard128():
    i = lax.broadcasted_iota(jnp.int32, (128, 128), 0)
    j = lax.broadcasted_iota(jnp.int32, (128, 128), 1)
    v = i & j
    v = v ^ (v >> 4)
    v = v ^ (v >> 2)
    v = v ^ (v >> 1)
    return (1 - 2 * (v & 1)).astype(F32).astype(BF16)


def kernel(
    deltas, bits, tiles, counts, params, momentum,
    new_params, new_momentum, out,
    a_buf, s_buf, r_buf, w_buf, e_buf, q_out, q_in, g_out, g_in, sign_in, signs, weights, p_in, m_in,
    a_ss, a_rs, r_ss, r_rs, w_ss, e_rs, ag_ss, ag_rs, f_ss, f_rs, q_ss, q_rs, g_ss, g_rs, l_sem,
):
    x, c, y, z = place()
    half = x // 4
    quarter = x % 4
    pair = quarter // 2

    loads = [
        pltpu.make_async_copy(bits.at[pl.ds(pl.multiple_of(x // 4 * 8, 8), 8), pl.ds(pl.multiple_of(z * 1024, 1024), 1024)], sign_in, l_sem.at[0]),
        pltpu.make_async_copy(params, p_in, l_sem.at[1]),
        pltpu.make_async_copy(momentum, m_in, l_sem.at[2]),
    ]
    for load in loads:
        load.start()

    barrier = pltpu.get_barrier_semaphore()

    def greet(device):
        pl.semaphore_signal(barrier, inc=1, device_id=device, device_id_type=MESH)

    def greet_y(i):
        p = (2 * y + c + i) % 16
        greet(at(x, p % 2, p // 2, z))

    def greet_x(i):
        greet(at((x + i) % 8, c, y, z))

    def greet_z(i):
        p = (z * 8 + quarter * 2 + c + i) % 64
        greet(at(4 * half + p % 8 // 2, p % 2, y, p // 8))

    loop(1, 16, greet_y)
    loop(1, 8, greet_x)
    loop(1, 64, greet_z)
    stays = ((4 * half + y % 4) == x) & ((y // 2) == quarter)
    for t in range(2):
        own = (4 * half + y % 4 == x) & (2 * quarter + t == y)

        @pl.when(jnp.logical_not(own))
        def _():
            greet(at(4 * half + y % 4, c, 2 * quarter + t, z))

        own_in = (4 * half + y // 2 == x) & (quarter + 4 * t == y)

        @pl.when(jnp.logical_not(own_in))
        def _():
            greet(at(4 * half + y // 2, c, quarter + 4 * t, z))

    pl.semaphore_wait(barrier, 15 + 7 + 63 + 4 - 2 * stays.astype(jnp.int32))

    def y_peer(i):
        k = 8 + (2 * (i % 2) - 1) * ((i + 1) // 2)
        p = (2 * y + c + k) % 16
        return p // 2, p % 2

    def y_copy(j, i):
        py, pc = y_peer(i)
        return pltpu.make_async_remote_copy(
            src_ref=deltas.at[pl.ds(NZ * j, NZ), py, :, pc],
            dst_ref=a_buf.at[j, y, c],
            send_sem=a_ss.at[j, i],
            recv_sem=a_rs.at[j],
            device_id=at(x, pc, py, z),
            device_id_type=MESH,
        )

    def send_y(j):
        loop(0, 15, lambda i: y_copy(j, i).start())
        pltpu.make_async_copy(deltas.at[pl.ds(NZ * j, NZ), y, :, c], a_buf.at[j, y, c], a_rs.at[j]).start()

    send_y(0)
    send_y(1)

    loads[1].wait()
    loads[2].wait()
    for n in range(32):
        both = [
            p_in[:, (2 * n + t) * 128 : (2 * n + t + 1) * 128] - 0.567 * m_in[:, (2 * n + t) * 128 : (2 * n + t + 1) * 128]
            for t in range(2)
        ]
        q_out[n // 4, n % 4] = jnp.concatenate(both, axis=0)

    def q_target(i):
        pz = (z + i // 4) % 8
        m = i % 4
        return pz, m, (4 * half + m == x) & (pair == c) & (pz == z)

    def q_copy(i):
        pz, m, _ = q_target(i)
        return pltpu.make_async_remote_copy(
            src_ref=q_out.at[pz, m],
            dst_ref=q_in.at[z, x % 2, c],
            send_sem=q_ss.at[i],
            recv_sem=q_rs,
            device_id=at(4 * half + m, pair, y, pz),
            device_id_type=MESH,
        )

    def q_send(i):
        pz, m, own = q_target(i)

        @pl.when(jnp.logical_not(own))
        def _():
            q_copy(i).start()

        @pl.when(own)
        def _():
            pltpu.make_async_copy(q_out.at[pz, m], q_in.at[z, x % 2, c], q_rs).start()

    def q_done(i):
        @pl.when(jnp.logical_not(q_target(i)[2]))
        def _():
            q_copy(i).wait_send()

    loop(0, 32, q_send)

    loads[0].wait()
    lane = lax.broadcasted_iota(jnp.int32, (8, MOST), 1)
    wanted = lax.broadcasted_iota(jnp.int32, (8, MOST), 0) + 8 * z
    for s in range(2):
        row = sign_in[pl.ds(2 * x % 8 + s, 1), :]
        for k in range(8):
            signs[s, k : k + 1, :] = (1 - 2 * row[:, k * 128 : (k + 1) * 128]).astype(F32)
        count = counts[2 * x + s]
        kept = (tiles[pl.ds(2 * x + s, 1), :] == wanted) & (lane < count)
        mask = jnp.sum(kept.astype(F32), axis=1, keepdims=True)
        factor = (64.0 / 32.0) / jnp.full((8, 128), count, jnp.int32).astype(F32)
        weights[s] = mask * factor

    h128 = hadamard128()

    def rotate(parts):
        stacked = jnp.concatenate([parts[k][s] for k in range(8) for s in range(2)], axis=0)
        full = jnp.dot(stacked, h128, preferred_element_type=F32)
        return [[full[(2 * k + s) * 32 : (2 * k + s + 1) * 32] for s in range(2)] for k in range(8)]

    def columns(lists, f):
        sides = [f(s, [lists[k][s] for k in range(8)]) for s in range(2)]
        return [[sides[s][k] for s in range(2)] for k in range(8)]

    def compute(j):
        def group(i):
            flipped = [
                [(a_buf[j, k, s, i].reshape(32, 128).astype(F32) * signs[s, k : k + 1, :]).astype(BF16) for s in range(2)]
                for k in range(8)
            ]

            def middle(s, v):
                v = butterfly(v)
                return [(v[k] * weights[s, k : k + 1, :]).astype(BF16) for k in range(8)]

            def last(s, v):
                v = butterfly(v)
                return [v[k] * (signs[s, k : k + 1, :] * (1.0 / 512.0)) for k in range(8)]

            back = columns(rotate(columns(rotate(flipped), middle)), last)
            for k in range(8):
                s_buf[j, k, i] = (back[k][0] + back[k][1]).astype(BF16).reshape(2, 16, 128)

        loop(0, NZ, group)

    def x_copy(j, i):
        px = (x + 4 + (2 * (i % 2) - 1) * ((i + 1) // 2)) % 8
        return pltpu.make_async_remote_copy(
            src_ref=s_buf.at[j, pl.ds(2 * (px % 4), 2), :, px // 4],
            dst_ref=r_buf.at[j, x],
            send_sem=r_ss.at[j, i],
            recv_sem=r_rs.at[j],
            device_id=at(px, c, y, z),
            device_id_type=MESH,
        )

    def send_x(j):
        loop(0, 7, lambda i: x_copy(j, i).start())
        pltpu.make_async_copy(s_buf.at[j, pl.ds(2 * quarter, 2), :, half], r_buf.at[j, x], r_rs.at[j]).start()

    def g_target(j, i):
        zr = NZ * j + i // 4
        tx = 4 * half + 2 * c + i % 4 // 2
        tc = i % 2
        return zr, tx, tc, (zr == z) & (tx == x) & (tc == c)

    def g_copy(j, i):
        zr, tx, tc, _ = g_target(j, i)
        return pltpu.make_async_remote_copy(
            src_ref=g_out.at[zr, i % 4],
            dst_ref=g_in.at[z, quarter],
            send_sem=g_ss.at[j, i],
            recv_sem=g_rs,
            device_id=at(tx, tc, y, zr),
            device_id_type=MESH,
        )

    def g_send(j, i):
        zr, _, _, own = g_target(j, i)

        @pl.when(jnp.logical_not(own))
        def _():
            g_copy(j, i).start()

        @pl.when(own)
        def _():
            pltpu.make_async_copy(g_out.at[zr, i % 4], g_in.at[z, quarter], g_rs).start()

    def g_done(j, i):
        @pl.when(jnp.logical_not(g_target(j, i)[3]))
        def _():
            g_copy(j, i).wait_send()

    def w_own(t):
        return (4 * half + y % 4 == x) & (2 * quarter + t == y)

    def w_copy(j, t):
        return pltpu.make_async_remote_copy(
            src_ref=w_buf.at[j, t],
            dst_ref=e_buf.at[j, :, y // 4],
            send_sem=w_ss.at[j, t],
            recv_sem=e_rs.at[j],
            device_id=at(4 * half + y % 4, c, 2 * quarter + t, z),
            device_id_type=MESH,
        )

    def update(j):
        pltpu.make_async_copy(r_buf.at[j], r_buf.at[j], r_rs.at[j]).wait()
        for i in range(NZ):
            g = []
            for t in range(2):
                total = r_buf[j, 0, t, i].astype(F32)
                for n in range(1, 8):
                    total = total + r_buf[j, n, t, i].astype(F32)
                g.append(total)
            ws = [[], []]
            for xr in range(2):
                mixed = []
                for cr in range(2):
                    low = 8 * xr + 4 * cr
                    packed = jnp.concatenate([g[t][low : low + 4] for t in range(2)], axis=0)
                    g_out[NZ * j + i, 2 * xr + cr] = packed
                    mixed.append(q_in[NZ * j + i, xr, cr] - 1.33 * packed)
                for t in range(2):
                    ws[t] += [mixed[cr][4 * t : 4 * t + 4] for cr in range(2)]
            for t in range(2):
                w_buf[j, t, i] = jnp.concatenate(ws[t], axis=0).astype(BF16)
        for t in range(2):
            own = w_own(t)

            @pl.when(jnp.logical_not(own))
            def _():
                w_copy(j, t).start()

            @pl.when(own)
            def _():
                pltpu.make_async_copy(w_buf.at[j, t], e_buf.at[j, :, y // 4], e_rs.at[j]).start()

        loop(0, 4 * NZ, lambda i: g_send(j, i))

    def ag_copy(j, i):
        px = (x + 4 + (2 * (i % 2) - 1) * ((i + 1) // 2)) % 8
        return pltpu.make_async_remote_copy(
            src_ref=e_buf.at[j],
            dst_ref=out.at[pl.ds(NZ * j, NZ), :, quarter, half, c],
            send_sem=ag_ss.at[j, i],
            recv_sem=ag_rs.at[j],
            device_id=at(px, c, y, z),
            device_id_type=MESH,
        )

    def gather(j):
        pltpu.make_async_copy(e_buf.at[j], e_buf.at[j], e_rs.at[j]).wait()
        loop(0, 7, lambda i: ag_copy(j, i).start())
        pltpu.make_async_copy(e_buf.at[j], out.at[pl.ds(NZ * j, NZ), :, quarter, half, c], ag_rs.at[j]).start()

    def sibling(j):
        part = out.at[pl.ds(NZ * j, NZ), :, :, :, c]
        return pltpu.make_async_remote_copy(
            src_ref=part, dst_ref=part, send_sem=f_ss.at[j], recv_sem=f_rs.at[j],
            device_id=at(x, 1 - c, y, z), device_id_type=MESH,
        )

    def forward(j):
        part = out.at[pl.ds(NZ * j, NZ), :, :, :, c]
        pltpu.make_async_copy(part, part, ag_rs.at[j]).wait()
        sibling(j).start()

    for step in range(CHUNKS + 3):
        if step < CHUNKS:
            pltpu.make_async_copy(a_buf.at[step], a_buf.at[step], a_rs.at[step]).wait()
            if step + 2 < CHUNKS:
                send_y(step + 2)
            compute(step)
            send_x(step)
        if 0 <= step - 1 < CHUNKS:
            if step == 1:
                pltpu.make_async_copy(q_in, q_in, q_rs).wait()
            update(step - 1)
        if 0 <= step - 2 < CHUNKS:
            gather(step - 2)
        if step == CHUNKS + 1:
            pltpu.make_async_copy(g_in, g_in, g_rs).wait()
            for n in range(32):
                both = g_in[n // 4, n % 4]
                for t in range(2):
                    cols = slice((2 * n + t) * 128, (2 * n + t + 1) * 128)
                    g = both[4 * t : 4 * t + 4]
                    m = 0.9 * m_in[:, cols] + g
                    new_momentum[:, cols] = m
                    new_params[:, cols] = p_in[:, cols] - 0.7 * (g + 0.9 * m)
        if 0 <= step - 3 < CHUNKS:
            forward(step - 3)

    for j in range(CHUNKS):
        loop(0, 15, lambda i: y_copy(j, i).wait_send())
        loop(0, 7, lambda i: x_copy(j, i).wait_send())
        loop(0, 7, lambda i: ag_copy(j, i).wait_send())
        loop(0, 4 * NZ, lambda i: g_done(j, i))
        for t in range(2):

            @pl.when(jnp.logical_not(w_own(t)))
            def _():
                w_copy(j, t).wait_send()

    loop(0, 32, q_done)
    for j in range(CHUNKS):
        sibling(j).wait_send()
        part = out.at[pl.ds(NZ * j, NZ), :, :, :, 1 - c]
        pltpu.make_async_copy(part, part, f_rs.at[j]).wait()


def body(deltas, sign_bits, kept_tiles, kept_count, params, momentum):
    anywhere = pl.BlockSpec(memory_space=pl.ANY)
    vmem = pl.BlockSpec(memory_space=pltpu.VMEM)
    new_params, new_momentum, working = pl.pallas_call(
        kernel,
        out_shape=(
            jax.ShapeDtypeStruct(params.shape, F32),
            jax.ShapeDtypeStruct(params.shape, F32),
            jax.ShapeDtypeStruct((8, 2, 4, 2, 2, 16, 128), BF16),
        ),
        in_specs=[anywhere, anywhere, vmem, pl.BlockSpec(memory_space=pltpu.SMEM), anywhere, anywhere],
        out_specs=(vmem, vmem, anywhere),
        scratch_shapes=[
            pltpu.VMEM((CHUNKS, 8, 2, NZ, 2, 16, 128), BF16),
            pltpu.VMEM((CHUNKS, 8, NZ, 2, 16, 128), BF16),
            pltpu.VMEM((CHUNKS, 8, 2, NZ, 16, 128), BF16),
            pltpu.VMEM((CHUNKS, 2, NZ, 16, 128), BF16),
            pltpu.VMEM((CHUNKS, NZ, 2, 16, 128), BF16),
            pltpu.VMEM((8, 4, 8, 128), F32),
            pltpu.VMEM((8, 2, 2, 8, 128), F32),
            pltpu.VMEM((8, 4, 8, 128), F32),
            pltpu.VMEM((8, 4, 8, 128), F32),
            pltpu.VMEM((8, 1024), jnp.int32),
            pltpu.VMEM((2, 8, 128), F32),
            pltpu.VMEM((2, 8, 128), F32),
            pltpu.VMEM(params.shape, F32),
            pltpu.VMEM(params.shape, F32),
            DMA((CHUNKS, 15)),
            DMA((CHUNKS,)),
            DMA((CHUNKS, 7)),
            DMA((CHUNKS,)),
            DMA((CHUNKS, 2)),
            DMA((CHUNKS,)),
            DMA((CHUNKS, 7)),
            DMA((CHUNKS,)),
            DMA((CHUNKS,)),
            DMA((CHUNKS,)),
            DMA((32,)),
            DMA,
            DMA((CHUNKS, 4 * NZ)),
            DMA,
            DMA((3,)),
        ],
        compiler_params=pltpu.CompilerParams(
            collective_id=0, has_side_effects=True, vmem_limit_bytes=32 * 2**20
        ),
    )(deltas.reshape(8, 8, 2, 2, 16, 128), sign_bits, kept_tiles, kept_count, params, momentum)
    return new_params, new_momentum, working.reshape(4096, 128)


def solution(mesh):
    placed = (P("rep", None, "fsdp"), P(), P(), P(), P(("fsdp", "rep"), None), P(("fsdp", "rep"), None))
    return jax.shard_map(
        body,
        mesh=mesh,
        in_specs=placed,
        out_specs=(P(("fsdp", "rep"), None), P(("fsdp", "rep"), None), P(None, "fsdp")),
        check_vma=False,
    )
```

time: 324 us -> 81.1 us (0.25)
  waiting for transfers between devices: 192 us -> 0 us
  Pallas kernels: 0 us -> 72.4 us
  blocking collectives: 41.7 us -> 0 us
  other arithmetic: 27.5 us -> 0 us
  starting transfers between devices: 24.4 us -> 0 us
  between operations: 14.8 us -> 0.65 us
  matrix products: 8.19 us -> 0 us
  local copies, waits for them, and re-layouts: 14.3 us -> 7.7 us
    unnamed x3 -> x0, waiting for transfers between devices: 121 us -> none
    pallas_call x0 -> x1, Pallas kernels: none -> 72.4 us  [body(): pl.pallas_call(kernel, out_shape=(jax.ShapeDtypeStruct(params.shape, F32)...]
    all_gather x1 -> x0, waiting for transfers between devices: 46.7 us -> none  [body(): gathered = lax.all_gather(working, 'rep', axis=0, tiled=True)]
    all_to_all x1 -> x0, blocking collectives: 41.7 us -> none  [body(): lax.all_to_all(gathered, 'fsdp', split_axis=1, concat_axis=0, tiled=True)]
    all_to_all x1 -> x0, waiting for transfers between devices: 24.4 us -> none  [body(): lax.all_to_all(deltas, 'fsdp', split_axis=1, concat_axis=2, tiled=True)]
    unnamed x2 -> x0, other arithmetic: 24.2 us -> none
    all_to_all x1 -> x0, starting transfers between devices: 24 us -> none  [body(): lax.all_to_all(deltas, 'fsdp', split_axis=1, concat_axis=2, tiled=True)]
    dot_general x1 -> x0, matrix products: 8.19 us -> none  [body(): jnp.einsum('nbi,ij->nbj', kept, rotation, preferred_element_type=jnp.floa...]
  transfers between devices with their start and end apart: 3 -> 0, of which waited for: 3 -> 0; matrix products, arithmetic and copies ran while one was open for 1% -> 0% of each run, Pallas kernels for 0% -> 0%
where the time goes in v1:
time: 81.1 us; the launch traced here: 80.8 us
  Pallas kernels  72.4 us (89%)
  local copies, waits for them, and re-layouts  7.7 us (9%)
    pallas_call x1, Pallas kernels, body(): pl.pallas_call(kernel, out_shape=(jax.ShapeDtypeStruct(params.shape, F32)...  72.4 us
    unnamed x15, local copies, waits for them, and re-layouts  7.7 us

profile of v1, /device:TPU:1, one launch (start us, length us, event | category | flops | bytes accessed | tf_op | source)
XLA Modules:
  0.0 80.8 jit_solution(10029263620092487360)
XLA Ops:
  0.6 0.0 copy-start.5
  0.6 0.6 copy-done.5
  1.3 0.0 copy-start
  1.3 1.2 %copy-done = bf16[1,4096,128]{2,1,0:T(8,128)(2,1)S(1)} copy-done((bf16[1,4096,128]{2,1,0:T(8,128)(2,1)S(1)}, bf16[1,4096,128]{2,1,0:T(8,128)(2,1)}, u32[]{:S(2)}) %copy-start) | copy-done | bytes 1048600
  2.5 0.0 copy-start.1
  2.5 1.0 %copy-done.1 = s32[16,8192]{1,0:T(8,128)S(1)} copy-done((s32[16,8192]{1,0:T(8,128)S(1)}, s32[16,8192]{1,0:T(8,128)}, u32[]{:S(2)}) %copy-start.1) | copy-done | bytes 524312
  3.6 0.0 copy-start.2
  3.6 0.9 %copy-done.2 = f32[4,8192]{1,0:T(4,128)S(1)} copy-done((f32[4,8192]{1,0:T(4,128)S(1)}, f32[4,8192]{1,0:T(4,128)}, u32[]{:S(2)}) %copy-start.2) | copy-done | bytes 131096
  4.5 0.0 copy-start.3
  4.5 0.9 %copy-done.3 = f32[4,8192]{1,0:T(4,128)S(1)} copy-done((f32[4,8192]{1,0:T(4,128)S(1)}, f32[4,8192]{1,0:T(4,128)}, u32[]{:S(2)}) %copy-start.3) | copy-done | bytes 131096
  5.4 0.0 copy-start.4
  5.4 0.7 copy-done.4
  6.1 72.4 %shard_map.85 = (f32[4,8192]{1,0:T(4,128)S(1)}, f32[4,8192]{1,0:T(4,128)S(1)}, bf16[8,2,4,2,2,16,128]{6,5,4,3,2,1,0:T(8,128)(2,1)S(1)}) custom-call(bf16[8,8,2,2,16,128]{5,4,3,2,1,0:T(8,128)(2,1)S(1)} %bitcast.2, s32[16,8192]{1,0:T(8,128)S(1)} %copy-done.1, s32[16,32]{1,0:T(8,128)S(1)} %copy-done.4, s32[16]{0:T(128)S(1)} %copy-done.5, ...), custom_call_target="tpu_custom_call" | custom-call | tf_op jit(solution)/shard_map/pallas_call | solution.py:386
  78.5 0.7 copy.12
  79.1 0.7 copy.13
  79.8 1.0 %copy.14 = bf16[4096,128]{1,0:T(8,128)(2,1)} copy(bf16[4096,128]{1,0:T(8,128)(2,1)S(1)} %bitcast.3) | data formatting | bytes 2097152
Async XLA Ops:
  0.6 0.7 copy-start.5
  1.3 1.2 %copy-start = (bf16[1,4096,128]{2,1,0:T(8,128)(2,1)S(1)}, bf16[1,4096,128]{2,1,0:T(8,128)(2,1)}, u32[]{:S(2)}) copy-start(bf16[1,4096,128]{2,1,0:T(8,128)(2,1)} %param.6) | copy-start | bytes 3145732
  2.5 1.0 %copy-start.1 = (s32[16,8192]{1,0:T(8,128)S(1)}, s32[16,8192]{1,0:T(8,128)}, u32[]{:S(2)}) copy-start(s32[16,8192]{1,0:T(8,128)} %bits.1) | copy-start | bytes 1572868
  3.6 0.9 %copy-start.2 = (f32[4,8192]{1,0:T(4,128)S(1)}, f32[4,8192]{1,0:T(4,128)}, u32[]{:S(2)}) copy-start(f32[4,8192]{1,0:T(4,128)} %params.1) | copy-start | bytes 393220
  4.5 0.9 %copy-start.3 = (f32[4,8192]{1,0:T(4,128)S(1)}, f32[4,8192]{1,0:T(4,128)}, u32[]{:S(2)}) copy-start(f32[4,8192]{1,0:T(4,128)} %momentum.1) | copy-start | bytes 393220
  5.4 0.7 copy-start.4

commit v2 on v1

v2 whole, which is shorter than its diff:
```python
import jax
import jax.numpy as jnp
from jax import lax
from jax.experimental import pallas as pl
from jax.experimental.pallas import tpu as pltpu
from jax.sharding import PartitionSpec as P

MESH = pl.DeviceIdType.MESH
DMA = pltpu.SemaphoreType.DMA
CHUNKS = 4
NZ = 8 // CHUNKS
MOST = 32
F32 = jnp.float32
BF16 = jnp.bfloat16


def place():
    rep = lax.axis_index("rep")
    col = lax.axis_index("fsdp")
    return rep >> 1, rep & 1, col & 7, col >> 3


def at(x, c, y, z):
    return (2 * x + c, 8 * z + y)


def loop(low, high, body):
    def step(i, carry):
        body(i)
        return carry

    lax.fori_loop(low, high, step, jnp.int32(0))


def butterfly(v):
    for bit in (1, 2, 4):
        v = [v[i] + v[i | bit] if not i & bit else v[i ^ bit] - v[i] for i in range(8)]
    return v


def hadamard128():
    i = lax.broadcasted_iota(jnp.int32, (128, 128), 0)
    j = lax.broadcasted_iota(jnp.int32, (128, 128), 1)
    v = i & j
    v = v ^ (v >> 4)
    v = v ^ (v >> 2)
    v = v ^ (v >> 1)
    return (1 - 2 * (v & 1)).astype(F32).astype(BF16)


def kernel(
    deltas, bits, tiles, counts, params, momentum,
    new_params, new_momentum, out,
    a_buf, s_buf, r_buf, w_buf, e_buf, full, q_out, q_in, g_out, g_in, sign_in, tiles_in, counts_in, signs, weights, p_in, m_in,
    a_ss, a_rs, r_ss, r_rs, w_ss, e_rs, ag_ss, ag_rs, f_ss, f_rs, q_ss, q_rs, g_ss, g_rs, l_sem,
):
    x, c, y, z = place()
    half = x >> 2
    quarter = x & 3
    pair = quarter >> 1

    loads = [
        pltpu.make_async_copy(bits.at[pl.ds(pl.multiple_of(half * 8, 8), 8), pl.ds(pl.multiple_of(z * 1024, 1024), 1024)], sign_in, l_sem.at[0]),
        pltpu.make_async_copy(params, p_in, l_sem.at[1]),
        pltpu.make_async_copy(momentum, m_in, l_sem.at[2]),
        pltpu.make_async_copy(tiles, tiles_in, l_sem.at[3]),
        pltpu.make_async_copy(counts, counts_in, l_sem.at[4]),
    ]
    for load in loads:
        load.start()

    barrier = pltpu.get_barrier_semaphore()

    def greet(device):
        pl.semaphore_signal(barrier, inc=1, device_id=device, device_id_type=MESH)

    def greet_y(i):
        p = (2 * y + c + i) & 15
        greet(at(x, p & 1, p >> 1, z))

    def greet_x(i):
        greet(at((x + i) & 7, c, y, z))

    def greet_z(i):
        p = (z * 8 + quarter * 2 + c + i) & 63
        greet(at(4 * half + ((p & 7) >> 1), p & 1, y, p >> 3))

    loop(1, 16, greet_y)
    loop(1, 8, greet_x)
    loop(1, 64, greet_z)
    stays = ((4 * half + (y & 3)) == x) & (((y >> 1)) == quarter)
    for t in range(2):
        own = (4 * half + (y & 3) == x) & (2 * quarter + t == y)

        @pl.when(jnp.logical_not(own))
        def _():
            greet(at(4 * half + (y & 3), c, 2 * quarter + t, z))

        own_in = (4 * half + (y >> 1) == x) & (quarter + 4 * t == y)

        @pl.when(jnp.logical_not(own_in))
        def _():
            greet(at(4 * half + (y >> 1), c, quarter + 4 * t, z))

    pl.semaphore_wait(barrier, 15 + 7 + 63 + 4 - 2 * stays.astype(jnp.int32))

    def y_peer(i):
        k = 8 + (2 * (i & 1) - 1) * ((i + 1) >> 1)
        p = (2 * y + c + k) & 15
        return p >> 1, p & 1

    def y_copy(j, i):
        py, pc = y_peer(i)
        return pltpu.make_async_remote_copy(
            src_ref=deltas.at[pl.ds(NZ * j, NZ), py, :, pc],
            dst_ref=a_buf.at[j, 2 * y + c],
            send_sem=a_ss.at[j],
            recv_sem=a_rs.at[j],
            device_id=at(x, pc, py, z),
            device_id_type=MESH,
        )

    def send_y(j):
        loop(0, 15, lambda i: y_copy(j, i).start())
        pltpu.make_async_copy(deltas.at[pl.ds(NZ * j, NZ), y, :, c], a_buf.at[j, 2 * y + c], a_rs.at[j]).start()

    send_y(0)

    loads[1].wait()
    loads[2].wait()
    for n in range(32):
        both = [
            p_in[:, (2 * n + t) * 128 : (2 * n + t + 1) * 128] - 0.567 * m_in[:, (2 * n + t) * 128 : (2 * n + t + 1) * 128]
            for t in range(2)
        ]
        q_out[n // 4, n % 4] = jnp.concatenate(both, axis=0)

    def q_target(i):
        pz = (z + (i >> 2)) & 7
        m = i & 3
        return pz, m, (4 * half + m == x) & (pair == c) & (pz == z)

    def q_copy(i):
        pz, m, _ = q_target(i)
        return pltpu.make_async_remote_copy(
            src_ref=q_out.at[pz, m],
            dst_ref=q_in.at[z, x & 1, c],
            send_sem=q_ss,
            recv_sem=q_rs,
            device_id=at(4 * half + m, pair, y, pz),
            device_id_type=MESH,
        )

    def q_send(i):
        pz, m, own = q_target(i)

        @pl.when(jnp.logical_not(own))
        def _():
            q_copy(i).start()

        @pl.when(own)
        def _():
            pltpu.make_async_copy(q_out.at[pz, m], q_in.at[z, x & 1, c], q_rs).start()

    loop(0, 32, q_send)
    for j in range(1, CHUNKS):
        send_y(j)

    loads[0].wait()
    loads[3].wait()
    loads[4].wait()
    lane = lax.broadcasted_iota(jnp.int32, (8, MOST), 1)
    wanted = lax.broadcasted_iota(jnp.int32, (8, MOST), 0) + 8 * z
    for s in range(2):
        row = sign_in[pl.ds(2 * quarter + s, 1), :]
        for k in range(8):
            signs[s, k : k + 1, :] = (1 - 2 * row[:, k * 128 : (k + 1) * 128]).astype(F32)
        count = counts_in[2 * x + s]
        kept = (tiles_in[pl.ds(2 * x + s, 1), :] == wanted) & (lane < count)
        mask = jnp.sum(kept.astype(F32), axis=1, keepdims=True)
        factor = (64.0 / 32.0) / jnp.full((8, 128), count, jnp.int32).astype(F32)
        weights[s] = mask * factor

    h128 = hadamard128()

    def rotate(parts):
        stacked = jnp.concatenate([parts[k][s] for k in range(8) for s in range(2)], axis=0)
        full = jnp.dot(stacked, h128, preferred_element_type=F32)
        return [[full[(2 * k + s) * 32 : (2 * k + s + 1) * 32] for s in range(2)] for k in range(8)]

    def columns(lists, f):
        sides = [f(s, [lists[k][s] for k in range(8)]) for s in range(2)]
        return [[sides[s][k] for s in range(2)] for k in range(8)]

    def compute(j):
        def group(i):
            flipped = [
                [(a_buf[j, 2 * k + s, i].reshape(32, 128).astype(F32) * signs[s, k : k + 1, :]).astype(BF16) for s in range(2)]
                for k in range(8)
            ]

            def middle(s, v):
                v = butterfly(v)
                return [(v[k] * weights[s, k : k + 1, :]).astype(BF16) for k in range(8)]

            def last(s, v):
                v = butterfly(v)
                return [v[k] * (signs[s, k : k + 1, :] * (1.0 / 512.0)) for k in range(8)]

            back = columns(rotate(columns(rotate(flipped), middle)), last)
            for k in range(8):
                both = (back[k][0] + back[k][1]).astype(BF16).reshape(2, 16, 128)
                for h in range(2):
                    s_buf[j, h, k, i] = both[h]

        loop(0, NZ, group)

    def x_copy(j, i):
        px = (x + 4 + (2 * (i & 1) - 1) * ((i + 1) >> 1)) & 7
        return pltpu.make_async_remote_copy(
            src_ref=s_buf.at[j, px >> 2, pl.ds(2 * (px & 3), 2)],
            dst_ref=r_buf.at[j, x],
            send_sem=r_ss.at[j],
            recv_sem=r_rs.at[j],
            device_id=at(px, c, y, z),
            device_id_type=MESH,
        )

    def send_x(j):
        loop(0, 7, lambda i: x_copy(j, i).start())
        pltpu.make_async_copy(s_buf.at[j, half, pl.ds(2 * quarter, 2)], r_buf.at[j, x], r_rs.at[j]).start()

    def g_target(j, i):
        zr = NZ * j + (i >> 2)
        tx = 4 * half + 2 * c + ((i & 3) >> 1)
        tc = i & 1
        return zr, tx, tc, (zr == z) & (tx == x) & (tc == c)

    def g_copy(j, i):
        zr, tx, tc, _ = g_target(j, i)
        return pltpu.make_async_remote_copy(
            src_ref=g_out.at[4 * zr + (i & 3)],
            dst_ref=g_in.at[z, quarter],
            send_sem=g_ss,
            recv_sem=g_rs,
            device_id=at(tx, tc, y, zr),
            device_id_type=MESH,
        )

    def g_send(j, i):
        zr, _, _, own = g_target(j, i)

        @pl.when(jnp.logical_not(own))
        def _():
            g_copy(j, i).start()

        @pl.when(own)
        def _():
            pltpu.make_async_copy(g_out.at[4 * zr + (i & 3)], g_in.at[z, quarter], g_rs).start()

    def w_own(t):
        return (4 * half + (y & 3) == x) & (2 * quarter + t == y)

    def w_copy(j, t):
        return pltpu.make_async_remote_copy(
            src_ref=w_buf.at[j, t],
            dst_ref=e_buf.at[j, y >> 2],
            send_sem=w_ss.at[j, t],
            recv_sem=e_rs.at[j],
            device_id=at(4 * half + (y & 3), c, 2 * quarter + t, z),
            device_id_type=MESH,
        )

    def update(j):
        pltpu.make_async_copy(r_buf.at[j], r_buf.at[j], r_rs.at[j]).wait()
        for i in range(NZ):
            g = []
            for t in range(2):
                total = r_buf[j, 0, t, i].astype(F32)
                for n in range(1, 8):
                    total = total + r_buf[j, n, t, i].astype(F32)
                g.append(total)
            ws = [[], []]
            for xr in range(2):
                mixed = []
                for cr in range(2):
                    low = 8 * xr + 4 * cr
                    packed = jnp.concatenate([g[t][low : low + 4] for t in range(2)], axis=0)
                    g_out[4 * (NZ * j + i) + 2 * xr + cr] = packed
                    mixed.append(q_in[NZ * j + i, xr, cr] - 1.33 * packed)
                for t in range(2):
                    ws[t] += [mixed[cr][4 * t : 4 * t + 4] for cr in range(2)]
            for t in range(2):
                w_buf[j, t, i] = jnp.concatenate(ws[t], axis=0).astype(BF16)
        for t in range(2):
            own = w_own(t)

            @pl.when(jnp.logical_not(own))
            def _():
                w_copy(j, t).start()

            @pl.when(own)
            def _():
                pltpu.make_async_copy(w_buf.at[j, t], e_buf.at[j, y >> 2], e_rs.at[j]).start()

        loop(0, 4 * NZ, lambda i: g_send(j, i))

    def ag_copy(j, i):
        px = (x + 4 + (2 * (i & 1) - 1) * ((i + 1) >> 1)) & 7
        return pltpu.make_async_remote_copy(
            src_ref=e_buf.at[j],
            dst_ref=full.at[j, c, x],
            send_sem=ag_ss.at[j],
            recv_sem=ag_rs.at[j],
            device_id=at(px, c, y, z),
            device_id_type=MESH,
        )

    def gather(j):
        pltpu.make_async_copy(e_buf.at[j], e_buf.at[j], e_rs.at[j]).wait()
        loop(0, 7, lambda i: ag_copy(j, i).start())
        pltpu.make_async_copy(e_buf.at[j], full.at[j, c, x], ag_rs.at[j]).start()

    def sibling(j):
        part = full.at[j, c]
        return pltpu.make_async_remote_copy(
            src_ref=part, dst_ref=part, send_sem=f_ss.at[j], recv_sem=f_rs.at[j],
            device_id=at(x, 1 - c, y, z), device_id_type=MESH,
        )

    def forward(j):
        part = full.at[j, c]
        pltpu.make_async_copy(part, part, ag_rs.at[j]).wait()
        sibling(j).start()

    def arrange(j, side):
        def one(n):
            for s in range(2):
                for i in range(NZ):
                    out[NZ * j + i, s, n & 3, n >> 2, side] = full[j, side, n, s, i]

        loop(0, 8, one)

    def finish(j):
        pltpu.make_async_copy(full.at[j, 1 - c], full.at[j, 1 - c], f_rs.at[j]).wait()
        arrange(j, 1 - c)

    for step in range(CHUNKS + 3):
        if step < CHUNKS:
            pltpu.make_async_copy(a_buf.at[step], a_buf.at[step], a_rs.at[step]).wait()
            compute(step)
            send_x(step)
        if 0 <= step - 1 < CHUNKS:
            if step == 1:
                pltpu.make_async_copy(q_in, q_in, q_rs).wait()
            update(step - 1)
        if 0 <= step - 2 < CHUNKS:
            gather(step - 2)
        if step == CHUNKS + 1:
            pltpu.make_async_copy(g_in, g_in, g_rs).wait()
            for n in range(32):
                both = g_in[n // 4, n % 4]
                for t in range(2):
                    cols = slice((2 * n + t) * 128, (2 * n + t + 1) * 128)
                    g = both[4 * t : 4 * t + 4]
                    m = 0.9 * m_in[:, cols] + g
                    new_momentum[:, cols] = m
                    new_params[:, cols] = p_in[:, cols] - 0.7 * (g + 0.9 * m)
        if 0 <= step - 3 < CHUNKS:
            forward(step - 3)
            arrange(step - 3, c)

    def drain(ref, sem):
        pltpu.make_async_copy(ref, ref, sem).wait()

    for j in range(CHUNKS):
        drain(a_buf.at[j, pl.ds(0, 15)], a_ss.at[j])
        drain(r_buf.at[j, pl.ds(0, 7)], r_ss.at[j])
        drain(r_buf.at[j, pl.ds(0, 7)], ag_ss.at[j])
        for t in range(2):

            @pl.when(jnp.logical_not(w_own(t)))
            def _():
                w_copy(j, t).wait_send()

    mine = pair == c

    @pl.when(mine)
    def _():
        drain(g_out.at[pl.ds(0, 31)], g_ss)
        drain(g_out.at[pl.ds(0, 31)], q_ss)

    @pl.when(jnp.logical_not(mine))
    def _():
        drain(g_out, g_ss)
        drain(g_out, q_ss)

    for j in range(CHUNKS):
        sibling(j).wait_send()
        finish(j)


def body(deltas, sign_bits, kept_tiles, kept_count, params, momentum):
    anywhere = pl.BlockSpec(memory_space=pl.ANY)
    vmem = pl.BlockSpec(memory_space=pltpu.VMEM)
    new_params, new_momentum, working = pl.pallas_call(
        kernel,
        out_shape=(
            jax.ShapeDtypeStruct(params.shape, F32),
            jax.ShapeDtypeStruct(params.shape, F32),
            jax.ShapeDtypeStruct((8, 2, 4, 2, 2, 16, 128), BF16),
        ),
        in_specs=[anywhere] * 6,
        out_specs=(vmem, vmem, vmem),
        scratch_shapes=[
            pltpu.VMEM((CHUNKS, 16, NZ, 2, 16, 128), BF16),
            pltpu.VMEM((CHUNKS, 2, 8, NZ, 16, 128), BF16),
            pltpu.VMEM((CHUNKS, 8, 2, NZ, 16, 128), BF16),
            pltpu.VMEM((CHUNKS, 2, NZ, 16, 128), BF16),
            pltpu.VMEM((CHUNKS, 2, NZ, 16, 128), BF16),
            pltpu.VMEM((CHUNKS, 2, 8, 2, NZ, 16, 128), BF16),
            pltpu.VMEM((8, 4, 8, 128), F32),
            pltpu.VMEM((8, 2, 2, 8, 128), F32),
            pltpu.VMEM((32, 8, 128), F32),
            pltpu.VMEM((8, 4, 8, 128), F32),
            pltpu.VMEM((8, 1024), jnp.int32),
            pltpu.VMEM((16, MOST), jnp.int32),
            pltpu.SMEM((16,), jnp.int32),
            pltpu.VMEM((2, 8, 128), F32),
            pltpu.VMEM((2, 8, 128), F32),
            pltpu.VMEM(params.shape, F32),
            pltpu.VMEM(params.shape, F32),
            DMA((CHUNKS,)),
            DMA((CHUNKS,)),
            DMA((CHUNKS,)),
            DMA((CHUNKS,)),
            DMA((CHUNKS, 2)),
            DMA((CHUNKS,)),
            DMA((CHUNKS,)),
            DMA((CHUNKS,)),
            DMA((CHUNKS,)),
            DMA((CHUNKS,)),
            DMA,
            DMA,
            DMA,
            DMA,
            DMA((5,)),
        ],
        compiler_params=pltpu.CompilerParams(
            collective_id=0, has_side_effects=True, vmem_limit_bytes=60 * 2**20
        ),
    )(deltas.reshape(8, 8, 2, 2, 16, 128), sign_bits, kept_tiles, kept_count, params, momentum)
    return new_params, new_momentum, working.reshape(4096, 128)


def solution(mesh):
    placed = (P("rep", None, "fsdp"), P(), P(), P(), P(("fsdp", "rep"), None), P(("fsdp", "rep"), None))
    return jax.shard_map(
        body,
        mesh=mesh,
        in_specs=placed,
        out_specs=(P(("fsdp", "rep"), None), P(("fsdp", "rep"), None), P(None, "fsdp")),
        check_vma=False,
    )
```

time: 81.1 us -> 76.1 us (0.938)
  local copies, waits for them, and re-layouts: 7.7 us -> 4.52 us
  Pallas kernels: 72.4 us -> 70.7 us
    unnamed x15 -> x5, local copies, waits for them, and re-layouts: 7.7 us -> 4.52 us
    pallas_call x1, Pallas kernels: 72.4 us -> 70.7 us  [body(): pl.pallas_call(kernel, out_shape=(jax.ShapeDtypeStruct(params.shape, F32)...]
where the time goes in v2:
time: 76.1 us; the launch traced here: 75.9 us
  Pallas kernels  70.7 us (93%)
  local copies, waits for them, and re-layouts  4.52 us (6%)
    pallas_call x1, Pallas kernels, body(): pl.pallas_call(kernel, out_shape=(jax.ShapeDtypeStruct(params.shape, F32)...  70.7 us
    unnamed x5, local copies, waits for them, and re-layouts  4.52 us

profile of v2, /device:TPU:1, one launch (start us, length us, event | category | flops | bytes accessed | tf_op | source)
XLA Modules:
  0.0 75.9 jit_solution(17821134625191911417)
XLA Ops:
  0.6 70.7 %shard_map.85 = (f32[4,8192]{1,0:T(4,128)}, f32[4,8192]{1,0:T(4,128)}, bf16[8,2,4,2,2,16,128]{6,5,4,3,2,1,0:T(8,128)(2,1)}) custom-call(bf16[8,8,2,2,16,128]{5,4,3,2,1,0:T(8,128)(2,1)} %bitcast.2, s32[16,8192]{1,0:T(8,128)} %bits.1, s32[16,32]{1,0:T(8,128)} %tiles.1, s32[16]{0:T(128)} %counts.1, f32[4,8192]{1,0:T(4,128)} %params.1, f32[4,8192]{1,0:T(4,128)} %momentum.1), custom_call_target="tpu_custom_call" | custom-call | tf_op jit(solution)/shard_map/pallas_call | solution.py:406
  71.4 0.0 copy-start
  71.4 1.6 %copy.12 = f32[4,8192]{1,0:T(4,128)} copy(f32[4,8192]{1,0:T(4,128)} %get-tuple-element.12) | data formatting | bytes 262144
  73.0 0.0 copy-done
  73.0 0.7 copy.13
  73.6 2.3 %copy.14 = bf16[4096,128]{1,0:T(8,128)(2,1)} copy(bf16[4096,128]{1,0:T(8,128)(2,1)} %bitcast.3) | data formatting | bytes 2097152
Async XLA Ops:
  71.4 1.6 %copy-start = (f32[4,8192]{1,0:T(4,128)S(1)}, f32[4,8192]{1,0:T(4,128)}, u32[]{:S(2)}) copy-start(f32[4,8192]{1,0:T(4,128)} %get-tuple-element.13) | copy-start | bytes 393220

commit v3 on v2

--- a/solution.py
+++ b/solution.py
@@ -7,7 +7,7 @@
 
 MESH = pl.DeviceIdType.MESH
 DMA = pltpu.SemaphoreType.DMA
-CHUNKS = 4
+CHUNKS = 2
 NZ = 8 // CHUNKS
 MOST = 32
 F32 = jnp.float32

time: 76.1 us -> 82.5 us (1.084)
  Pallas kernels: 70.7 us -> 77.1 us
    pallas_call x1, Pallas kernels: 70.7 us -> 77.1 us  [body(): pl.pallas_call(kernel, out_shape=(jax.ShapeDtypeStruct(params.shape, F32)...]
where the time goes in v3:
time: 82.5 us; the launch traced here: 82.3 us
  Pallas kernels  77.1 us (93%)
  local copies, waits for them, and re-layouts  4.52 us (5%)
    pallas_call x1, Pallas kernels, body(): pl.pallas_call(kernel, out_shape=(jax.ShapeDtypeStruct(params.shape, F32)...  77.1 us
    unnamed x5, local copies, waits for them, and re-layouts  4.52 us

profile of v3, /device:TPU:1, one launch (start us, length us, event | category | flops | bytes accessed | tf_op | source)
XLA Modules:
  0.0 82.3 jit_solution(3888574637281731236)
XLA Ops:
  0.6 77.1 %shard_map.85 = (f32[4,8192]{1,0:T(4,128)}, f32[4,8192]{1,0:T(4,128)}, bf16[8,2,4,2,2,16,128]{6,5,4,3,2,1,0:T(8,128)(2,1)}) custom-call(bf16[8,8,2,2,16,128]{5,4,3,2,1,0:T(8,128)(2,1)} %bitcast.2, s32[16,8192]{1,0:T(8,128)} %bits.1, s32[16,32]{1,0:T(8,128)} %tiles.1, s32[16]{0:T(128)} %counts.1, f32[4,8192]{1,0:T(4,128)} %params.1, f32[4,8192]{1,0:T(4,128)} %momentum.1), custom_call_target="tpu_custom_call" | custom-call | tf_op jit(solution)/shard_map/pallas_call | solution.py:406
  77.8 0.0 copy-start
  77.8 1.6 %copy.12 = f32[4,8192]{1,0:T(4,128)} copy(f32[4,8192]{1,0:T(4,128)} %get-tuple-element.12) | data formatting | bytes 262144
  79.4 0.0 copy-done
  79.4 0.7 copy.13
  80.0 2.3 %copy.14 = bf16[4096,128]{1,0:T(8,128)(2,1)} copy(bf16[4096,128]{1,0:T(8,128)(2,1)} %bitcast.3) | data formatting | bytes 2097152
Async XLA Ops:
  77.8 1.6 %copy-start = (f32[4,8192]{1,0:T(4,128)S(1)}, f32[4,8192]{1,0:T(4,128)}, u32[]{:S(2)}) copy-start(f32[4,8192]{1,0:T(4,128)} %get-tuple-element.13) | copy-start | bytes 393220
